TPU v7x, 32 devices: a whole 2x2x4 slice. The times are simulated.
32 devices in a mesh: row: 4 (over y, core), col: 8 (over z, x).
Axes of the slice: x: 2, y: 2, z: 4, core: 2. Of those that a mesh axis runs over, the one named last changes fastest.
Arguments:
- stored: float32 [16384, 16384], P('row', 'col'), may hold values from -1 to 2.5, as said below
Outputs:
- factored: float32 [16384, 16384], P('row', 'col')
Inputs may be any that keep to these rules, and one draw needn't show every extreme that they name: `stored`: symmetric positive definite with smallest eigenvalue at least 0.25: a Rotne-Prager-Yamakawa mobility of beads of unit radius (3 x 3 blocks per pair, correlation-regularized, self-mobility scaled to 1; the last rows beyond a multiple of 3 are unit diagonal) with perturbed off-diagonal entries, plus a positive diagonal.
All inputs are finite; a program needn't handle non-finite values.
Results may differ from a plain program's by a relative error of at most 0.0001.
Values sent between devices are 32-bit elements; how exact they have to be, the bound alone decides.
No kernel may reach another device: no remote copies, remote signals or barrier semaphores. Data moves between devices by JAX's collectives and lax.ppermute only.
A program may use at most 192 MiB of HBM per device.

v0:
```python
import jax
import jax.numpy as jnp
from jax import lax
from jax.sharding import PartitionSpec as P

NB = 256
PANELS = 2


def from_root(array, axis, root):
    mine = lax.axis_index(axis) == root
    return lax.psum(jnp.where(mine, array, jnp.zeros_like(array)), axis)


def factor_panel(diag, block, row_ids, panel, owning):
    width = diag.shape[0]
    safe = jnp.where(owning, diag, jnp.eye(width, dtype=jnp.float32))
    lower = jnp.linalg.cholesky(safe)
    solved = jax.scipy.linalg.solve_triangular(lower, block.T, lower=True).T
    tiles = solved.reshape(-1, width, width)
    picked = jnp.where(
        (row_ids > panel)[:, None, None],
        tiles,
        jnp.where((row_ids == panel)[:, None, None], lower[None], jnp.float32(0.0)),
    )
    return picked.reshape(-1, width)


def local(stored):
    rows_axis = lax.axis_size("row")
    cols_axis = lax.axis_size("col")
    my_row = lax.axis_index("row")
    my_col = lax.axis_index("col")
    width = NB
    rtiles = stored.shape[0] // width
    ctiles = stored.shape[1] // width
    row_ids = my_row + rows_axis * jnp.arange(rtiles, dtype=jnp.int32)
    col_ids = my_col + cols_axis * jnp.arange(ctiles, dtype=jnp.int32)
    work = stored
    for panel in range(PANELS):
        base = panel // cols_axis * width
        diag_base = panel // rows_axis * width
        column_block = work[:, base : base + width]
        owning = my_col == panel % cols_axis
        diag = from_root(column_block[diag_base : diag_base + width], "row", panel % rows_axis)
        local_panel = factor_panel(diag, column_block, row_ids, panel, owning)
        rows_panel = from_root(local_panel, "col", panel % cols_axis)
        tiles = rows_panel.reshape(rtiles, width, width)
        picks = []
        for slot in range(ctiles):
            source = (my_col + cols_axis * slot) // rows_axis
            picks.append(lax.dynamic_index_in_dim(tiles, source, 0, keepdims=False))
        chosen = jnp.stack(picks)
        mirrored = from_root(chosen, "row", my_col % rows_axis)
        left = jnp.where((row_ids > panel)[:, None, None], tiles, jnp.float32(0.0)).reshape(
            -1, width
        )
        right = jnp.where((col_ids > panel)[:, None, None], mirrored, jnp.float32(0.0)).reshape(
            -1, width
        )
        update = lax.dot_general(
            left,
            right,
            (((1,), (1,)), ((), ())),
            precision=lax.Precision.HIGHEST,
            preferred_element_type=jnp.float32,
        )
        work = work - update
        column_new = jnp.where(owning, rows_panel, work[:, base : base + width])
        work = work.at[:, base : base + width].set(column_new)
    upper = (row_ids < PANELS)[:, None] & (col_ids >= PANELS)[None, :]
    blocks = work.reshape(rtiles, width, ctiles, width)
    blocks = jnp.where(upper[:, None, :, None], jnp.float32(0.0), blocks)
    return blocks.reshape(rtiles * width, ctiles * width)


def solution(mesh):
    placed = (P("row", "col"),)
    return jax.shard_map(
        local, mesh=mesh, in_specs=placed, out_specs=P("row", "col"), check_vma=False
    )
```

profile of v0, /device:TPU:24, one launch (start us, length us, event | category | flops | bytes accessed | tf_op | source)
XLA Modules:
  0.0 852.7 jit_solution(10245656014689485188)
XLA Ops:
  6.5 31.1 %copy.5 = f32[4096,2048]{0,1:T(8,128)} copy(f32[4096,2048]{1,0:T(8,128)} %param.8) | data formatting | bytes 67108864 | tf_op args[0]
  43.9 28.5 %all-reduce.8.cloned.1.call-done = f32[256,256]{0,1:T(8,128)} async-done(((f32[256,256]{0,1:T(8,128)}), f32[256,256]{0,1:T(8,128)}) %all-reduce.8.cloned.1.call-update) | async-done | bytes 262160 | tf_op jit(solution)/shard_map/psum | solution.py:12
  72.7 11.7 %cholesky.130 = f32[128,128]{1,0:T(8,128)S(1)} custom-call(f32[128,128]{1,0:T(8,128)S(1)} %cholesky.194), custom_call_target="Cholesky" | custom-call | tf_op jit(solution)/shard_map/jit(cholesky)/cholesky | solution.py:18
  84.4 9.8 %custom-call.13 = f32[1,128,128]{1,2,0:T(8,128)S(1)} custom-call(f32[1,128,128]{2,1,0:T(8,128)S(1)} %get-tuple-element.96), custom_call_target="InvertDiagBlocksLowerTriangular" | custom-call | tf_op jit(solution)/shard_map/jit(cholesky)/cholesky | solution.py:18
  94.7 11.7 %cholesky.147 = f32[128,128]{1,0:T(8,128)S(1)} custom-call(f32[128,128]{1,0:T(8,128)S(1)} %convolution_subtract_fusion.5), custom_call_target="Cholesky" | custom-call | tf_op jit(solution)/shard_map/jit(cholesky)/cholesky | solution.py:18
  108.8 5.9 copy.14
  118.9 19.7 %custom-call.14 = f32[2,128,128]{1,2,0:T(8,128)S(1)} custom-call(f32[2,128,128]{2,1,0:T(8,128)S(1)} %get-tuple-element.45), custom_call_target="InvertDiagBlocksLowerTriangular" | custom-call | tf_op jit(solution)/shard_map/jit(_solve_triangular)/triangular_solve | solution.py:19
  151.3 153.5 %all-reduce.10.cloned.1.call-done = f32[4096,256]{0,1:T(8,128)} async-done(((f32[4096,256]{0,1:T(8,128)}), f32[4096,256]{0,1:T(8,128)}) %all-reduce.10.cloned.1.call-update) | async-done | bytes 4194320 | tf_op jit(solution)/shard_map/psum | solution.py:12
  319.0 52.3 %all-reduce.12.cloned.1.call-done = f32[8,256,256]{1,0,2:T(8,128)} async-done(((f32[8,256,256]{1,0,2:T(8,128)}), f32[8,256,256]{1,0,2:T(8,128)}) %all-reduce.12.cloned.1.call-update) | async-done | bytes 2097168 | tf_op jit(solution)/shard_map/psum | solution.py:12
  374.2 33.9 %convolution_subtract_fusion.1 = f32[4096,2048]{0,1:T(8,128)} fusion(f32[4096,2048]{0,1:T(8,128)} %copy.5, f32[2048,256]{0,1:T(8,128)S(1)} %bitcast.123, f32[4096,256]{0,1:T(8,128)S(1)} %copy-done.1, pred[4096]{0:T(1024)(128)(4,1)S(1)} %broadcast_in_dim.124), kind=kOutput, calls=%fused_computation.6 | convolution fusion | flops 25779240960 | bytes 73404416 | tf_op jit(solution)/shard_map/dot_general | solution.py:61
  408.0 5.5 constant_dynamic-update-slice_fusion.2
  416.7 31.8 %all-reduce.14.cloned.1.call-done = f32[256,256]{0,1:T(8,128)} async-done(((f32[256,256]{0,1:T(8,128)}), f32[256,256]{0,1:T(8,128)}) %all-reduce.14.cloned.1.call-update) | async-done | bytes 262160 | tf_op jit(solution)/shard_map/psum | solution.py:12
  448.8 11.7 %cholesky.164 = f32[128,128]{1,0:T(8,128)S(1)} custom-call(f32[128,128]{1,0:T(8,128)S(1)} %cholesky.197), custom_call_target="Cholesky" | custom-call | tf_op jit(solution)/shard_map/jit(cholesky)/cholesky | solution.py:18
  460.5 9.8 %custom-call.15 = f32[1,128,128]{1,2,0:T(8,128)S(1)} custom-call(f32[1,128,128]{2,1,0:T(8,128)S(1)} %get-tuple-element.92), custom_call_target="InvertDiagBlocksLowerTriangular" | custom-call | tf_op jit(solution)/shard_map/jit(cholesky)/cholesky | solution.py:18
  470.8 11.7 %cholesky.181 = f32[128,128]{1,0:T(8,128)S(1)} custom-call(f32[128,128]{1,0:T(8,128)S(1)} %convolution_subtract_fusion.4), custom_call_target="Cholesky" | custom-call | tf_op jit(solution)/shard_map/jit(cholesky)/cholesky | solution.py:18
  485.5 6.2 copy.17
  495.5 19.7 %custom-call.16 = f32[2,128,128]{1,2,0:T(8,128)S(1)} custom-call(f32[2,128,128]{2,1,0:T(8,128)S(1)} %get-tuple-element.46), custom_call_target="InvertDiagBlocksLowerTriangular" | custom-call | tf_op jit(solution)/shard_map/jit(_solve_triangular)/triangular_solve | solution.py:19
  525.9 153.8 %all-reduce.16.cloned.1.call-done = f32[4096,256]{0,1:T(8,128)} async-done(((f32[4096,256]{0,1:T(8,128)}), f32[4096,256]{0,1:T(8,128)}) %all-reduce.16.cloned.1.call-update) | async-done | bytes 4194320 | tf_op jit(solution)/shard_map/psum | solution.py:12
  698.8 8.7 %copy.13 = pred[256,8,16,256]{3,1,2,0:T(8,128)(4,1)} copy(pred[256,8,16,256]{3,2,1,0:T(8,128)(4,1)} %bitcast.113) | data formatting | bytes 16777216
  707.4 38.8 %all-reduce.18.cloned.1.call-done = f32[8,256,256]{1,0,2:T(8,128)} async-done(((f32[8,256,256]{1,0,2:T(8,128)}), f32[8,256,256]{1,0,2:T(8,128)}) %all-reduce.18.cloned.1.call-update) | async-done | bytes 2097168 | tf_op jit(solution)/shard_map/psum | solution.py:12
  749.1 34.0 %convolution_subtract_fusion = f32[4096,2048]{0,1:T(8,128)} fusion(f32[4096,2048]{0,1:T(8,128)} %get-tuple-element.65, f32[2048,256]{0,1:T(8,128)S(1)} %bitcast.122, f32[4096,256]{0,1:T(8,128)S(1)} %copy-done, pred[4096]{0:T(1024)(128)(4,1)S(1)} %broadcast_in_dim.134), kind=kOutput, calls=%fused_computation.5 | convolution fusion | flops 25779240960 | bytes 73404416 | tf_op jit(solution)/shard_map/dot_general | solution.py:61
  783.1 5.5 fusion
  788.6 23.7 %broadcast_select_fusion = f32[4096,2048]{0,1:T(8,128)} fusion(pred[4096,2048]{0,1:T(8,128)(4,1)S(1)} %bitcast.112, f32[4096,2048]{0,1:T(8,128)} %fusion), kind=kLoop, calls=%fused_computation.4 | loop fusion | flops 8388608 | bytes 75497472 | tf_op jit(solution)/shard_map/jit(_where)/select_n | solution.py:73
  812.3 33.3 %copy.10 = f32[4096,2048]{1,0:T(8,128)} copy(f32[4096,2048]{0,1:T(8,128)} %broadcast_select_fusion) | data formatting | bytes 67108864 | tf_op jit(solution)/shard_map/jit(_where)/select_n | solution.py:73
  (116 shorter events, 91.9 us)
Async XLA Ops:
  6.5 65.9 %all-reduce.8.cloned.1.call-start = ((), (), s32[]{:S(2)}) async-start(), calls=%async_computation | async-start | bytes 524288 | tf_op jit(solution)/shard_map/psum | solution.py:12
  39.3 265.5 %all-reduce.10.cloned.1.call-start = ((), (), s32[]{:S(2)}) async-start(), calls=%async_computation.1 | async-start | bytes 8388608 | tf_op jit(solution)/shard_map/psum | solution.py:12
  138.6 3.7 copy-start.4
  142.3 5.5 copy-start.6
  150.8 220.5 %all-reduce.12.cloned.1.call-start = ((), (), s32[]{:S(2)}) async-start(), calls=%async_computation.2 | async-start | bytes 4194304 | tf_op jit(solution)/shard_map/psum | solution.py:12
  318.3 130.2 %all-reduce.14.cloned.1.call-start = ((), (), s32[]{:S(2)}) async-start(), calls=%async_computation.3 | async-start | bytes 524288 | tf_op jit(solution)/shard_map/psum | solution.py:12
  371.3 2.9 copy-start.1
  413.6 1.9 copy-start.2
  416.3 263.5 %all-reduce.16.cloned.1.call-start = ((), (), s32[]{:S(2)}) async-start(), calls=%async_computation.4 | async-start | bytes 8388608 | tf_op jit(solution)/shard_map/psum | solution.py:12
  515.2 3.7 copy-start.3
  518.9 3.9 copy-start.5
  525.7 220.5 %all-reduce.18.cloned.1.call-start = ((), (), s32[]{:S(2)}) async-start(), calls=%async_computation.5 | async-start | bytes 4194304 | tf_op jit(solution)/shard_map/psum | solution.py:12
  746.2 2.9 copy-start
  749.1 39.5 %slice-start = ((s8[8388608]{0:T(1024)(128)(4,1)}), s8[4194304]{0:T(1024)(128)(4,1)S(1)}, s32[]{:S(2)}) async-start(s8[8388608]{0:T(1024)(128)(4,1)} %bitcast.110), calls=%async_computation.6 | async-start | bytes 8388608
  749.1 39.5 %slice-start.1 = ((s8[8388608]{0:T(1024)(128)(4,1)}), s8[4194304]{0:T(1024)(128)(4,1)S(1)}, s32[]{:S(2)}) async-start(s8[8388608]{0:T(1024)(128)(4,1)} %bitcast.110), calls=%async_computation.7 | async-start | bytes 8388608
Sparse Core Ops, SparseCore 0:
  39.4 32.9 all-reduce.7
  150.9 153.8 all-reduce.9
  318.4 52.8 all-reduce.11
  416.4 32.0 all-reduce.13
  525.8 153.8 all-reduce.15
  693.3 52.8 all-reduce.17
where the time goes:
time: 866 us; the launch traced here: 853 us
  waiting for transfers between devices  459 us (53%)
  other arithmetic  159 us (18%)
  local copies, waits for them, and re-layouts  132 us (15%)
  matrix products  85.4 us (10%)
  between operations  16.4 us (2%)
    psum x6, waiting for transfers between devices, from_root(): return lax.psum(jnp.where(mine, array, jnp.zeros_like(array)), axis)  459 us
    another operation x13, other arithmetic, factor_panel(): lower = jnp.linalg.cholesky(safe)  68.5 us
    dot_general x2, matrix products, local(): lax.dot_general(left, right, (((1,), (1,)), ((), ())), precision=lax.Prec...  67.9 us
    unnamed x26, local copies, waits for them, and re-layouts  63.4 us
    another operation x5, other arithmetic, factor_panel(): solved = jax.scipy.linalg.solve_triangular(lower, block.T, lower=True).T  39.4 us
    select_n x1, local copies, waits for them, and re-layouts, local(): blocks = jnp.where(upper[:, None, :, None], jnp.float32(0.0), blocks)  33.3 us
    select_n x1, other arithmetic, local(): blocks = jnp.where(upper[:, None, :, None], jnp.float32(0.0), blocks)  23.7 us
  transfers between devices with their start and end apart: 6, of which 6 were waited for; matrix products, arithmetic and copies ran while one was open for 2% of the time, Pallas kernels for 0%

commit v1 on v0

v1 whole, which is shorter than its diff:
```python
import functools

import jax
import jax.numpy as jnp
from jax import lax
from jax.experimental import pallas as pl
from jax.experimental.pallas import tpu as pltpu
from jax.sharding import PartitionSpec as P

NB = 256
PANELS = 2
WIDE = PANELS * NB
STEP = 128
SUB = 8
ROOM = 58 * 2**20
HIGHEST = lax.Precision.HIGHEST
F32 = jnp.float32
BF16 = jnp.bfloat16


def any_spec():
    return pl.BlockSpec(memory_space=pl.ANY)


def dot(a, b, dims):
    return lax.dot_general(
        a, b, ((dims[0], dims[1]), ((), ())), precision=HIGHEST, preferred_element_type=F32
    )


def eliminate(work, start):
    rows = work[start : start + SUB, :]
    lanes = rows.shape[1]
    sub = lax.broadcasted_iota(jnp.int32, (SUB, STEP), 0)
    cols = [
        jnp.broadcast_to(rows[:, start + c : start + c + 1], (SUB, STEP)) for c in range(SUB)
    ]
    parts = [rows[:, a : a + STEP] for a in range(0, lanes, STEP)]
    for c in range(SUB):
        pivot = jnp.broadcast_to(cols[c][c : c + 1, :], (SUB, STEP))
        root = lax.rsqrt(pivot)
        root = root * (1.5 - 0.5 * pivot * root * root)
        factor = jnp.where(sub > c, cols[c] * root, 0.0)
        scale = jnp.where(sub == c, root, 1.0)

        def step(x, c=c, root=root, factor=factor, scale=scale):
            line = jnp.broadcast_to(x[c : c + 1, :], (SUB, STEP)) * root
            return x * scale - factor * line

        parts = [step(x) for x in parts]
        for d in range(c + 1, SUB):
            cols[d] = step(cols[d])
    return jnp.concatenate(parts, 1)


def factor_kernel(block, s_ref, u_in, v_in, u_ref, v_ref, work):
    lo, hi = block * STEP, (block + 1) * STEP
    u_ref[...] = u_in[...]
    v_ref[...] = v_in[...]
    row = s_ref[lo:hi, :]
    eye = (
        lax.broadcasted_iota(jnp.int32, (STEP, STEP), 0)
        == lax.broadcasted_iota(jnp.int32, (STEP, STEP), 1)
    ).astype(F32)
    if lo:
        left = u_in[0:lo, lo:hi]
        row = row - dot(left, u_in[0:lo, :], ((0,), (0,)))
        inv = -dot(left, v_in[0:lo, 0:lo], ((0,), (0,)))
    work[:, 0:STEP] = row[:, lo:hi]
    work[:, STEP:] = eye
    lanes = lax.broadcasted_iota(jnp.int32, (SUB, 2 * STEP), 1)
    for start in range(0, STEP, SUB):
        done = eliminate(work, start)
        work[start : start + SUB, :] = jnp.where(lanes >= start, done, 0.0)
        if start + SUB < STEP:
            rest = work[start + SUB :, :]
            work[start + SUB :, :] = rest - dot(
                done[:, start + SUB : STEP], done, ((0,), (0,))
            )
    dinv = work[:, STEP:]
    u_ref[lo:hi, lo:hi] = work[:, 0:STEP]
    v_ref[lo:hi, lo:hi] = dinv
    if hi < WIDE:
        u_ref[lo:hi, hi:] = dot(dinv, row[:, hi:], ((1,), (0,)))
    if lo:
        v_ref[lo:hi, 0:lo] = dot(dinv, inv, ((1,), (0,)))


def factor(block, s, u, v):
    return pl.pallas_call(
        functools.partial(factor_kernel, block),
        out_shape=[jax.ShapeDtypeStruct((WIDE, WIDE), F32)] * 2,
        scratch_shapes=[pltpu.VMEM((STEP, 2 * STEP), F32)],
        input_output_aliases={1: 0, 2: 1},
        compiler_params=pltpu.CompilerParams(vmem_limit_bytes=ROOM),
        cost_estimate=pl.CostEstimate(
            flops=6 * 10**9, bytes_accessed=6 * 2**20, transcendentals=0
        ),
        name="factor",
    )(s, u, v)


def split(x):
    high = x.astype(BF16)
    return high, (x - high.astype(F32)).astype(BF16)


def right_kernel(tab, v_ref, b_ref, hi_ref, lo_ref, sinv):
    mine, side = tab[0], tab[1]

    @pl.when(pl.program_id(0) == 0)
    def _():
        sinv[...] = dot(v_ref[...], v_ref[...], ((0,), (0,)))

    def place(k):
        return pl.ds(pl.multiple_of(lax.rem(k + PANELS - side, PANELS) * NB, NB), NB)

    for k in range(PANELS):
        high, low = split(dot(sinv[k * NB : (k + 1) * NB, :], b_ref[...], ((1,), (0,))))
        hi_ref[place(k), :] = high
        lo_ref[place(k), :] = low
    for j in range(PANELS):

        @pl.when((pl.program_id(0) == 0) & (mine == j))
        def _(j=j):
            for k in range(PANELS):
                high, low = split(-v_ref[j * NB : (j + 1) * NB, k * NB : (k + 1) * NB].T)
                hi_ref[place(k), 0:NB] = high
                lo_ref[place(k), 0:NB] = low


def right(tab, v, b):
    cols = b.shape[1]
    wide = min(cols, 512)
    return pl.pallas_call(
        right_kernel,
        grid_spec=pltpu.PrefetchScalarGridSpec(
            num_scalar_prefetch=1,
            grid=(cols // wide,),
            in_specs=[
                pl.BlockSpec((WIDE, WIDE), lambda c, t: (0, 0)),
                pl.BlockSpec((WIDE, wide), lambda c, t: (0, c)),
            ],
            out_specs=[pl.BlockSpec((WIDE, wide), lambda c, t: (0, c))] * 2,
            scratch_shapes=[pltpu.VMEM((WIDE, WIDE), F32)],
        ),
        out_shape=[jax.ShapeDtypeStruct((WIDE, cols), BF16)] * 2,
        compiler_params=pltpu.CompilerParams(vmem_limit_bytes=ROOM),
        cost_estimate=pl.CostEstimate(
            flops=12 * WIDE * WIDE * cols, bytes_accessed=10 * WIDE * cols, transcendentals=0
        ),
        name="right",
    )(tab, v, b)


def update_kernel(first, count, nbuf, tab, m_ref, hi_ref, lo_ref, *refs):
    own, other = refs[:nbuf], refs[nbuf : 2 * nbuf]
    out_ref, lhs, sem = refs[-3], refs[-2], refs[-1]
    s = pl.program_id(0)
    chain, mine, my_row = tab[0], tab[1], tab[2]

    def fetch(n, act):
        slot = lax.rem(n, 2)
        for x in range(nbuf):

            @pl.when(n + chain == x)
            def _(x=x):
                act(pltpu.make_async_copy(own[x], lhs.at[slot, 0], sem.at[slot, 0]))
                act(pltpu.make_async_copy(other[x], lhs.at[slot, 1], sem.at[slot, 1]))

    @pl.when(s == 0)
    def _():
        fetch(s, lambda c: c.start())

    @pl.when(s + 1 < count)
    def _():
        fetch(s + 1, lambda c: c.start())

    fetch(s, lambda c: c.wait())
    slot = lax.rem(s, 2)
    oh, ol = split(lhs[slot, 0])
    th, tl = split(lhs[slot, 1])
    left = jnp.concatenate([oh, th, oh, th, ol, tl], 1)
    cols = m_ref.shape[1]
    for a in range(0, cols, NB):
        rh, rl = hi_ref[:, a : a + NB], lo_ref[:, a : a + NB]
        prod = jnp.dot(
            left, jnp.concatenate([rh, rl, rh], 0), preferred_element_type=F32
        )
        m = m_ref[:, a : a + NB]
        if a == 0:
            m = jnp.where(mine < PANELS, 0.0, m)
        out_ref[:, a : a + NB] = m - prod
    if first == 0:

        @pl.when((s == 0) & (my_row < PANELS))
        def _():
            r = lax.broadcasted_iota(jnp.int32, (NB, NB), 0)
            c = lax.broadcasted_iota(jnp.int32, (NB, NB), 1)
            keep = (mine < PANELS) & ((my_row > mine) | ((my_row == mine) & (r >= c)))
            out_ref[0:NB, 0:NB] = jnp.where(keep, out_ref[0:NB, 0:NB], 0.0)
            if cols > NB:
                out_ref[0:NB, NB:] = jnp.zeros((NB, cols - NB), F32)


def update(tab, first, count, stored, high, low, own, other, prev):
    nrows, cols = stored.shape
    tall = own[0].shape[0]
    args = [stored, high, low, *own, *other] + ([] if prev is None else [prev])
    whole = pl.BlockSpec((WIDE, cols), lambda s, t: (0, 0), pipeline_mode=pl.Buffered(1))
    return pl.pallas_call(
        functools.partial(update_kernel, first, count, len(own)),
        grid_spec=pltpu.PrefetchScalarGridSpec(
            num_scalar_prefetch=1,
            grid=(count,),
            in_specs=[pl.BlockSpec((tall, cols), lambda s, t: (first + s, 0)), whole, whole]
            + [any_spec()] * (len(args) - 3),
            out_specs=pl.BlockSpec((tall, cols), lambda s, t: (first + s, 0)),
            scratch_shapes=[
                pltpu.VMEM((2, PANELS, tall, NB), F32),
                pltpu.SemaphoreType.DMA((2, PANELS)),
            ],
        ),
        out_shape=jax.ShapeDtypeStruct((nrows, cols), F32),
        input_output_aliases={} if prev is None else {len(args): 0},
        compiler_params=pltpu.CompilerParams(vmem_limit_bytes=ROOM),
        cost_estimate=pl.CostEstimate(
            flops=6 * count * tall * WIDE * cols,
            bytes_accessed=8 * count * tall * cols + 4 * WIDE * cols,
            transcendentals=0,
        ),
        name="update",
    )(tab, *args)


def after(x, *done):
    return lax.optimization_barrier((x, *done))[0]


def local(mesh, stored):
    rows, cols = mesh.shape["row"], mesh.shape["col"]
    layers, length = rows // PANELS, cols // PANELS
    both = ("row", "col")
    my_row, my_col = lax.axis_index("row"), lax.axis_index("col")
    layer, lane = my_row // PANELS, my_row % PANELS
    link, side = my_col // PANELS, my_col % PANELS
    rtiles = stored.shape[0] // NB
    tall = (2 if rtiles % 2 == 0 else 1) * NB
    pieces = stored.shape[0] // tall
    nsteps = pieces + length - 1
    devices = [
        (y, c, l, f)
        for y in range(layers)
        for c in range(PANELS)
        for l in range(length)
        for f in range(PANELS)
    ]

    def at(y, c, l, f):
        return (y * PANELS + c) * cols + l * PANELS + f

    def move(x, to):
        pairs = [(at(*d), at(*t)) for d in devices if (t := to(*d)) is not None]
        return lax.ppermute(x, both, pairs)

    def pair(flag, x, y, axis):
        return jnp.concatenate([jnp.where(flag, y, x), jnp.where(flag, x, y)], axis)

    corner = stored[0:NB, 0:NB]
    block = corner
    hops = [
        move(corner, lambda y, c, l, f, h=h: (y, c, h, f) if (y, l) == (0, 0) else None)
        for h in range(1, length)
    ]

    def panel(s):
        return stored[s * tall : (s + 1) * tall, 0:NB]

    own, other, along = [], [], None

    def send(s, *done):
        if s == 0:
            cur = panel(0)
        elif s < pieces:
            cur = jnp.where(link == 0, panel(s), along)
        else:
            cur = along
        if done:
            cur = after(cur, *done)
        own.append(cur)
        z = None
        if s < nsteps - 1:
            z = move(
                cur,
                lambda y, c, l, f: (y, c, l + 1, f)
                if 0 <= s - l < pieces and l + 1 < length
                else None,
            )
        other.append(
            move(cur, lambda y, c, l, f: (y, c, l, 1 - f) if 0 <= s - l < pieces else None)
        )
        return z

    along = send(0)
    for h, x in enumerate(hops):
        block = jnp.where(link == h + 1, x, block)
    near, far = block, block
    cross = move(block, lambda y, c, l, f: (y, c, l, 1 - f) if y == 0 else None)
    for h in range(1, layers):
        x = move(block, lambda y, c, l, f: (h, c, l, f) if y == 0 else None)
        y_ = move(block, lambda y, c, l, f: (h, c, l, 1 - f) if y == 0 else None)
        near = jnp.where(layer == h, x, near)
        cross = jnp.where(layer == h, y_, cross)
    line = pair(side == 1, near, cross, 1)
    s_all = pair(lane == 1, line, move(line, lambda y, c, l, f: (y, 1 - c, l, f)), 0)

    along = send(1)
    top = after(stored[0:NB, :], near, cross)
    cur, half = top, top
    for h in range(1, layers):
        cur = move(cur, lambda y, c, l, f: (h, c, l, f) if y == h - 1 else None)
        half = jnp.where(layer == h, cur, half)
    mate = move(half, lambda y, c, l, f: (y, 1 - c, l, f))

    flags = jnp.stack([link, my_col, my_row, side]).astype(jnp.int32)
    u = jnp.zeros((WIDE, WIDE), F32)
    v = jnp.zeros((WIDE, WIDE), F32)
    nblocks = WIDE // STEP
    start = min(3, nsteps - 1)
    out, rest = None, 0
    high = low = None
    todo = [("factor", k) for k in range(nblocks)] + [("right", 0)]
    for s in range(2, nsteps):
        dep = []
        if s > start and todo:
            kind, k = todo.pop(0)
            if kind == "factor":
                u, v = factor(k, after(s_all, own[s - 1]) if k == 0 else s_all, u, v)
                dep = [v]
            else:
                b = pair(lane == 1, half, mate, 0)
                high, low = right(jnp.stack([my_col, side]).astype(jnp.int32), v, b)
                dep = [low]
        elif s > start and high is not None:
            stop = min(rest + 2, s - length + 1, pieces)
            if stop > rest:
                out = run_update(flags, rest, stop, stored, high, low, own, other, out, length)
                rest = stop
                dep = [out]
        along = send(s, *dep, other[s - 2])
    for kind, k in todo:
        if kind == "factor":
            u, v = factor(k, s_all, u, v)
        else:
            b = pair(lane == 1, half, mate, 0)
            high, low = right(jnp.stack([my_col, side]).astype(jnp.int32), v, b)
    cuts = [x for x in (pieces - 2, pieces - 1, pieces) if x > rest]
    for stop in cuts:
        out = run_update(flags, rest, stop, stored, high, low, own, other, out, length)
        rest = stop
    return out


def run_update(flags, first, stop, stored, high, low, own, other, prev, length):
    lo, hi = first, stop + length - 1
    return update(
        flags, first, stop - first, stored, high, low, own[lo:hi], other[lo:hi], prev
    )


def solution(mesh):
    return jax.shard_map(
        functools.partial(local, mesh),
        mesh=mesh,
        in_specs=(P("row", "col"),),
        out_specs=P("row", "col"),
        check_vma=False,
    )
```

time: 866 us -> 248 us (0.29); the launches traced: 853 us -> 247 us
  waiting for transfers between devices: 459 us -> 46.6 us
  other arithmetic: 159 us -> 19.6 us
  Pallas kernels: 0 us -> 128 us
  local copies, waits for them, and re-layouts: 132 us -> 8.53 us
  matrix products: 85.4 us -> 0 us
  starting transfers between devices: 0.96 us -> 42.9 us
  between operations: 16.4 us -> 0.87 us
    psum x6 -> x0, waiting for transfers between devices: 459 us -> none  [from_root(): return lax.psum(jnp.where(mine, array, jnp.zeros_like(array)), axis)]
    pallas_call x0 -> x10, Pallas kernels: none -> 128 us  [the longest x5 65.8 us: update(): pl.pallas_call(functools.partial(update_kernel, first, count, len(own)),...]
    another operation x19 -> x2, other arithmetic: 109 us -> 1.15 us  [the longest x1 0.59 us: local(): flags = jnp.stack([link, my_col, my_row, side]).astype(jnp.int32)]
    dot_general x2 -> x0, matrix products: 67.9 us -> none  [local(): lax.dot_general(left, right, (((1,), (1,)), ((), ())), precision=lax.Prec...]
    unnamed x26 -> x40, local copies, waits for them, and re-layouts: 63.4 us -> 1.74 us
    ppermute x0 -> x30, waiting for transfers between devices: none -> 46.6 us  [move(): return lax.ppermute(x, both, pairs)]
    ppermute x0 -> x30, starting transfers between devices: none -> 42.9 us  [move(): return lax.ppermute(x, both, pairs)]
    select_n x5 -> x0, local copies, waits for them, and re-layouts: 33.8 us -> none  [the longest x1 33.3 us: local(): blocks = jnp.where(upper[:, None, :, None], jnp.float32(0.0), blocks)]
  transfers between devices with their start and end apart: 6 -> 30, of which waited for: 6 -> 5; matrix products, arithmetic and copies ran while one was open for 2% -> 10% of each run, Pallas kernels for 0% -> 48%
where the time goes in v1:
time: 248 us; the launch traced here: 247 us
  Pallas kernels  128 us (52%)
  waiting for transfers between devices  46.6 us (19%)
  starting transfers between devices  42.9 us (17%)
  other arithmetic  19.6 us (8%)
  local copies, waits for them, and re-layouts  8.53 us (3%)
    pallas_call x5, Pallas kernels, update(): pl.pallas_call(functools.partial(update_kernel, first, count, len(own)),...  65.8 us
    pallas_call x4, Pallas kernels, factor(): pl.pallas_call(functools.partial(factor_kernel, block), out_shape=[jax.Sh...  49.6 us
    ppermute x30, waiting for transfers between devices, move(): return lax.ppermute(x, both, pairs)  46.6 us
    ppermute x30, starting transfers between devices, move(): return lax.ppermute(x, both, pairs)  42.9 us
    pallas_call x1, Pallas kernels, right(): pl.pallas_call(right_kernel, grid_spec=pltpu.PrefetchScalarGridSpec(num_s...  12.8 us
    select_n x7, other arithmetic, send(): cur = jnp.where(link == 0, panel(s), along)  8.1 us
  transfers between devices with their start and end apart: 30, of which 5 were waited for; matrix products, arithmetic and copies ran while one was open for 10% of the time, Pallas kernels for 48%

profile of v1, /device:TPU:24, one launch (start us, length us, event | category | flops | bytes accessed | tf_op | source)
XLA Modules:
  0.0 246.8 jit_solution(1921568486512639602)
XLA Ops:
  0.0 1.9 slice.34.refs_0_
  8.4 1.7 slice.35
  10.1 14.0 %collective-permute-done = f32[256,256]{1,0:T(8,128)S(1)} collective-permute-done((f32[256,256]{1,0:T(8,128)S(1)}, f32[256,256]{1,0:T(8,128)S(1)}, u32[]{:S(2)}, u32[]{:S(2)}) %collective-permute-start) | collective-permute-done | bytes 262176 | tf_op jit(solution)/shard_map/ppermute | solution.py:264
  26.5 3.4 %collective-permute-start.4 = (f32[256,256]{1,0:T(8,128)S(1)}, f32[256,256]{1,0:T(8,128)S(1)}, u32[]{:S(2)}, u32[]{:S(2)}) collective-permute-start(f32[256,256]{1,0:T(8,128)S(1)} %select_select_fusion), channel_id=1, source_target_pairs={{0,1},{1,0},{2,3},{3,2},{4,5},{5,4},{6,7},{7,6},{8,9},{9,8},{10,11... | collective-permute-start | bytes 786440 | tf_op jit(solution)/shard_map/ppermute | solution.py:264
  33.1 4.8 %collective-permute-done.4 = f32[256,256]{1,0:T(8,128)S(1)} collective-permute-done((f32[256,256]{1,0:T(8,128)S(1)}, f32[256,256]{1,0:T(8,128)S(1)}, u32[]{:S(2)}, u32[]{:S(2)}) %collective-permute-start.4) | collective-permute-done | bytes 262176 | tf_op jit(solution)/shard_map/ppermute | solution.py:264
  38.0 5.1 %collective-permute-start.12 = (f32[256,2048]{1,0:T(8,128)S(1)}, f32[256,2048]{1,0:T(8,128)}, u32[]{:S(2)}, u32[]{:S(2)}) collective-permute-start(f32[256,2048]{1,0:T(8,128)S(1)} %slice.35), channel_id=1, source_target_pairs={{0,16},{1,17},{2,18},{3,19},{4,20},{5,21},{6,22},{7,23},{8,24},{9,... | collective-permute-start | bytes 6291464 | tf_op jit(solution)/shard_map/ppermute | solution.py:264
  51.2 18.5 %collective-permute-done.10 = f32[512,256]{1,0:T(8,128)} collective-permute-done((f32[512,256]{1,0:T(8,128)S(1)}, f32[512,256]{1,0:T(8,128)}, u32[]{:S(2)}, u32[]{:S(2)}) %collective-permute-start.10) | collective-permute-done | bytes 524320 | tf_op jit(solution)/shard_map/ppermute | solution.py:264
  75.1 12.1 %factor.4 = (f32[512,512]{1,0:T(8,128)}, f32[512,512]{1,0:T(8,128)}) custom-call(f32[512,512]{1,0:T(8,128)} %pad_maximum_fusion.1.s_ref, f32[512,512]{1,0:T(8,128)} %broadcast_1_u_in_v_in.2.u_in, f32[512,512]{1,0:T(8,128)} %broadcast_1_u_in_v_in.2.clone.v_in), custom_call_target="tpu_custom_call", output_to_operand_aliasing={{0}: (1, {}), {1}: (2, {})} | custom-call | flops 6000000000 | bytes 6291456 | tf_op jit(solution)/shard_map/factor/pallas_call | solution.py:90
  92.8 12.5 %factor.5 = (f32[512,512]{1,0:T(8,128)}, f32[512,512]{1,0:T(8,128)}) custom-call(f32[512,512]{1,0:T(8,128)} %pad_maximum_fusion.1.s_ref, f32[512,512]{1,0:T(8,128)} %get-tuple-element.28.u_in, f32[512,512]{1,0:T(8,128)} %get-tuple-element.29.v_in), custom_call_target="tpu_custom_call", output_to_operand_aliasing={{0}: (1, {}), {1}: (2, {})} | custom-call | flops 6000000000 | bytes 6291456 | tf_op jit(solution)/shard_map/factor/pallas_call | solution.py:90
  108.7 12.4 %factor.6 = (f32[512,512]{1,0:T(8,128)}, f32[512,512]{1,0:T(8,128)}) custom-call(f32[512,512]{1,0:T(8,128)} %pad_maximum_fusion.1.s_ref, f32[512,512]{1,0:T(8,128)} %get-tuple-element.30.u_in, f32[512,512]{1,0:T(8,128)} %get-tuple-element.31.v_in), custom_call_target="tpu_custom_call", output_to_operand_aliasing={{0}: (1, {}), {1}: (2, {})} | custom-call | flops 6000000000 | bytes 6291456 | tf_op jit(solution)/shard_map/factor/pallas_call | solution.py:90
  121.2 3.4 %collective-permute-done.18 = f32[512,256]{1,0:T(8,128)S(1)} collective-permute-done((f32[512,256]{1,0:T(8,128)S(1)}, f32[512,256]{1,0:T(8,128)S(1)}, u32[]{:S(2)}, u32[]{:S(2)}) %collective-permute-start.18) | collective-permute-done | bytes 524320 | tf_op jit(solution)/shard_map/ppermute | solution.py:264
  127.6 12.6 %factor.7 = (f32[512,512]{1,0:T(8,128)}, f32[512,512]{1,0:T(8,128)}) custom-call(f32[512,512]{1,0:T(8,128)} %pad_maximum_fusion.1.s_ref, f32[512,512]{1,0:T(8,128)} %get-tuple-element.32.u_in, f32[512,512]{1,0:T(8,128)} %get-tuple-element.33.v_in), custom_call_target="tpu_custom_call", output_to_operand_aliasing={{0}: (1, {}), {1}: (2, {})} | custom-call | flops 6000000000 | bytes 6291456 | tf_op jit(solution)/shard_map/factor/pallas_call | solution.py:90
  140.2 5.8 %collective-permute-done.20 = f32[512,256]{1,0:T(8,128)S(1)} collective-permute-done((f32[512,256]{1,0:T(8,128)S(1)}, f32[512,256]{1,0:T(8,128)S(1)}, u32[]{:S(2)}, u32[]{:S(2)}) %collective-permute-start.20) | collective-permute-done | bytes 524320 | tf_op jit(solution)/shard_map/ppermute | solution.py:264
  149.3 2.1 broadcast_select_fusion.2
  151.4 2.5 %pad_maximum_fusion.b_ref = f32[512,2048]{1,0:T(8,128)} fusion(f32[256,2048]{1,0:T(8,128)S(1)} %get-tuple-element.49, f32[256,2048]{1,0:T(8,128)S(1)} %get-tuple-element.48), kind=kLoop, calls=%fused_computation | loop fusion | flops 1048576 | bytes 8388608 | tf_op jit(solution)/shard_map/concatenate | solution.py:267
  153.9 12.8 %right.1 = (bf16[512,2048]{1,0:T(8,128)(2,1)}, bf16[512,2048]{1,0:T(8,128)(2,1)}) custom-call(s32[2]{0:T(128)} %pad_add_fusion.1.tab, f32[512,512]{1,0:T(8,128)} %get-tuple-element.34.v_ref, f32[512,2048]{1,0:T(8,128)} %pad_maximum_fusion.b_ref), custom_call_target="tpu_custom_call" | custom-call | flops 6442450944 | bytes 10485760 | tf_op jit(solution)/shard_map/right/pallas_call | solution.py:135
  168.1 3.4 %collective-permute-start.27 = (f32[512,256]{1,0:T(8,128)S(1)}, f32[512,256]{1,0:T(8,128)S(1)}, u32[]{:S(2)}, u32[]{:S(2)}) collective-permute-start(f32[512,256]{1,0:T(8,128)S(1)} %collective-permute-done.22.refs_4_.refs_2_.refs_1_), channel_id=1, source_target_pairs={{2,3},{3,2},{4,5},{5,4},{6,7},{7,6},{10,11},{11,10},{12,13},{13,12... | collective-permute-start | bytes 1572872 | tf_op jit(solution)/shard_map/ppermute | solution.py:264
  171.5 14.9 %update.5.refs_10_ = f32[4096,2048]{1,0:T(8,128)} custom-call(s32[4]{0:T(128)} %pad_add_fusion.tab, f32[4096,2048]{1,0:T(8,128)} %m_ref.9, bf16[512,2048]{1,0:T(8,128)(2,1)} %get-tuple-element.36.hi_ref, bf16[512,2048]{1,0:T(8,128)(2,1)} %get-tuple-element.37.lo_ref, f32[512,256]{1,0:T(8,128)} %slice.34.refs_0_, f32[512,256]{1,0:T(8,128)} %copy-done.16, ...), custom_call_target="tpu_custom_call" | custom-call | flops 6442450944 | bytes 20971520 | tf_op jit(solution)/shard_map/update/pallas_call | solution.py:211
  187.7 2.4 collective-permute-start.28
  190.2 14.7 %update.6.refs_10_ = f32[4096,2048]{1,0:T(8,128)} custom-call(s32[4]{0:T(128)} %pad_add_fusion.tab, f32[4096,2048]{1,0:T(8,128)} %m_ref.9, bf16[512,2048]{1,0:T(8,128)(2,1)} %get-tuple-element.36.hi_ref, bf16[512,2048]{1,0:T(8,128)(2,1)} %get-tuple-element.37.lo_ref, f32[512,256]{1,0:T(8,128)} %copy-done.8, ...), custom_call_target="tpu_custom_call", output_to_operand_aliasing={{}: (14, {})} | custom-call | flops 6442450944 | bytes 20971520 | tf_op jit(solution)/shard_map/update/pallas_call | solution.py:211
  205.0 3.7 %collective-permute-start.29 = (f32[512,256]{1,0:T(8,128)S(1)}, f32[512,256]{1,0:T(8,128)S(1)}, u32[]{:S(2)}, u32[]{:S(2)}) collective-permute-start(f32[512,256]{1,0:T(8,128)S(1)} %collective-permute-done.26.refs_3_), channel_id=1, source_target_pairs={{6,7},{7,6},{14,15},{15,14},{22,23},{23,22},{30,31},{31,30}} | collective-permute-start | bytes 1572872 | tf_op jit(solution)/shard_map/ppermute | solution.py:264
  208.7 14.7 %update.7.refs_8_ = f32[4096,2048]{1,0:T(8,128)} custom-call(s32[4]{0:T(128)} %pad_add_fusion.tab, f32[4096,2048]{1,0:T(8,128)} %m_ref.9, bf16[512,2048]{1,0:T(8,128)(2,1)} %get-tuple-element.36.hi_ref, bf16[512,2048]{1,0:T(8,128)(2,1)} %get-tuple-element.37.lo_ref, f32[512,256]{1,0:T(8,128)} %copy-done, ...), custom_call_target="tpu_custom_call", output_to_operand_aliasing={{}: (14, {})} | custom-call | flops 6442450944 | bytes 20971520 | tf_op jit(solution)/shard_map/update/pallas_call | solution.py:211
  224.3 10.8 %update.8.refs_8_ = f32[4096,2048]{1,0:T(8,128)} custom-call(s32[4]{0:T(128)} %pad_add_fusion.tab, f32[4096,2048]{1,0:T(8,128)} %m_ref.9, bf16[512,2048]{1,0:T(8,128)(2,1)} %get-tuple-element.36.hi_ref, bf16[512,2048]{1,0:T(8,128)(2,1)} %get-tuple-element.37.lo_ref, f32[512,256]{1,0:T(8,128)} %copy-done.1, ...), custom_call_target="tpu_custom_call", output_to_operand_aliasing={{}: (12, {})} | custom-call | flops 3221225472 | bytes 12582912 | tf_op jit(solution)/shard_map/update/pallas_call | solution.py:211
  235.9 10.8 %update.9 = f32[4096,2048]{1,0:T(8,128)} custom-call(s32[4]{0:T(128)} %pad_add_fusion.tab, f32[4096,2048]{1,0:T(8,128)} %m_ref.9, bf16[512,2048]{1,0:T(8,128)(2,1)} %get-tuple-element.36.hi_ref, bf16[512,2048]{1,0:T(8,128)(2,1)} %get-tuple-element.37.lo_ref, f32[512,256]{1,0:T(8,128)} %copy-done.2, ...), custom_call_target="tpu_custom_call", output_to_operand_aliasing={{}: (12, {})} | custom-call | flops 3221225472 | bytes 12582912 | tf_op jit(solution)/shard_map/update/pallas_call | solution.py:211
  (109 shorter events, 44.9 us)
Async XLA Ops:
  1.9 29.4 %collective-permute-start.7 = (f32[512,256]{1,0:T(8,128)}, f32[512,256]{1,0:T(8,128)S(1)}, u32[]{:S(2)}, u32[]{:S(2)}) collective-permute-start(f32[512,256]{1,0:T(8,128)} %slice.34.refs_0_), channel_id=1, source_target_pairs={{0,2},{1,3},{8,10},{9,11},{16,18},{17,19},{24,26},{25,27}} | collective-permute-start | bytes 1572872 | tf_op jit(solution)/shard_map/ppermute | solution.py:264
  3.5 20.6 %collective-permute-start = (f32[256,256]{1,0:T(8,128)S(1)}, f32[256,256]{1,0:T(8,128)S(1)}, u32[]{:S(2)}, u32[]{:S(2)}) collective-permute-start(f32[256,256]{1,0:T(8,128)S(1)} %slice.30), channel_id=1, source_target_pairs={{0,6},{1,7},{8,14},{9,15}} | collective-permute-start | bytes 786440 | tf_op jit(solution)/shard_map/ppermute | solution.py:264
  4.8 19.3 %collective-permute-start.1 = (f32[256,256]{1,0:T(8,128)S(1)}, f32[256,256]{1,0:T(8,128)S(1)}, u32[]{:S(2)}, u32[]{:S(2)}) collective-permute-start(f32[256,256]{1,0:T(8,128)S(1)} %slice.30), channel_id=1, source_target_pairs={{0,4},{1,5},{8,12},{9,13}} | collective-permute-start | bytes 786440 | tf_op jit(solution)/shard_map/ppermute | solution.py:264
  5.5 18.6 %collective-permute-start.2 = (f32[256,256]{1,0:T(8,128)S(1)}, f32[256,256]{1,0:T(8,128)}, u32[]{:S(2)}, u32[]{:S(2)}) collective-permute-start(f32[256,256]{1,0:T(8,128)S(1)} %slice.30), channel_id=1, source_target_pairs={{0,2},{1,3},{8,10},{9,11}} | collective-permute-start | bytes 786440 | tf_op jit(solution)/shard_map/ppermute | solution.py:264
  6.9 38.2 %collective-permute-start.9 = (f32[512,256]{1,0:T(8,128)}, f32[512,256]{1,0:T(8,128)}, u32[]{:S(2)}, u32[]{:S(2)}) collective-permute-start(f32[512,256]{1,0:T(8,128)} %slice.34.refs_0_), channel_id=1, source_target_pairs={{0,1},{1,0},{8,9},{9,8},{16,17},{17,16},{24,25},{25,24}} | collective-permute-start | bytes 1572872 | tf_op jit(solution)/shard_map/ppermute | solution.py:264
  38.0 53.3 %collective-permute-start.12 = (f32[256,2048]{1,0:T(8,128)S(1)}, f32[256,2048]{1,0:T(8,128)}, u32[]{:S(2)}, u32[]{:S(2)}) collective-permute-start(f32[256,2048]{1,0:T(8,128)S(1)} %slice.35), channel_id=1, source_target_pairs={{0,16},{1,17},{2,18},{3,19},{4,20},{5,21},{6,22},{7,23},{8,24},{9,... | collective-permute-start | bytes 6291464 | tf_op jit(solution)/shard_map/ppermute | solution.py:264
  45.1 24.6 %collective-permute-start.10 = (f32[512,256]{1,0:T(8,128)S(1)}, f32[512,256]{1,0:T(8,128)}, u32[]{:S(2)}, u32[]{:S(2)}) collective-permute-start(f32[512,256]{1,0:T(8,128)S(1)} %slice_select_fusion.5.refs_2_.refs_0_), channel_id=1, source_target_pairs={{0,2},{1,3},{2,4},{3,5},{4,6},{5,7},{8,10},{9,11},{10,12},{11,13},... | collective-permute-start | bytes 1572872 | tf_op jit(solution)/shard_map/ppermute | solution.py:264
  47.6 23.4 %collective-permute-start.11 = (f32[512,256]{1,0:T(8,128)}, f32[512,256]{1,0:T(8,128)S(1)}, u32[]{:S(2)}, u32[]{:S(2)}) collective-permute-start(f32[512,256]{1,0:T(8,128)} %copy-done.16), channel_id=1, source_target_pairs={{0,1},{1,0},{2,3},{3,2},{8,9},{9,8},{10,11},{11,10},{16,17},{17,16... | collective-permute-start | bytes 1572872 | tf_op jit(solution)/shard_map/ppermute | solution.py:264
  48.3 40.1 %collective-permute-start.15 = (f32[512,256]{1,0:T(8,128)S(1)}, f32[512,256]{1,0:T(8,128)S(1)}, u32[]{:S(2)}, u32[]{:S(2)}) collective-permute-start(f32[512,256]{1,0:T(8,128)S(1)} %slice_select_fusion.5.refs_2_.refs_0_), channel_id=1, source_target_pairs={{0,1},{1,0},{2,3},{3,2},{4,5},{5,4},{8,9},{9,8},{10,11},{11,10},{1... | collective-permute-start | bytes 1572872 | tf_op jit(solution)/shard_map/ppermute | solution.py:264
  72.3 34.3 %collective-permute-start.17 = (f32[512,256]{1,0:T(8,128)S(1)}, f32[512,256]{1,0:T(8,128)S(1)}, u32[]{:S(2)}, u32[]{:S(2)}) collective-permute-start(f32[512,256]{1,0:T(8,128)S(1)} %slice_select_fusion.6.refs_3_.refs_1_), channel_id=1, source_target_pairs={{0,1},{1,0},{2,3},{3,2},{4,5},{5,4},{6,7},{7,6},{8,9},{9,8},{10,11... | collective-permute-start | bytes 1572872 | tf_op jit(solution)/shard_map/ppermute | solution.py:264
  88.4 16.9 %collective-permute-start.16 = (f32[512,256]{1,0:T(8,128)S(1)}, f32[512,256]{1,0:T(8,128)}, u32[]{:S(2)}, u32[]{:S(2)}) collective-permute-start(f32[512,256]{1,0:T(8,128)S(1)} %slice_select_fusion.refs_4_.refs_2_.refs_0_), channel_id=1, source_target_pairs={{0,2},{1,3},{2,4},{3,5},{4,6},{5,7},{8,10},{9,11},{10,12},{11,13},... | collective-permute-start | bytes 1572872 | tf_op jit(solution)/shard_map/ppermute | solution.py:264
  89.7 36.0 %collective-permute-start.19 = (f32[512,256]{1,0:T(8,128)S(1)}, f32[512,256]{1,0:T(8,128)S(1)}, u32[]{:S(2)}, u32[]{:S(2)}) collective-permute-start(f32[512,256]{1,0:T(8,128)S(1)} %slice_select_fusion.refs_4_.refs_2_.refs_0_), channel_id=1, source_target_pairs={{0,1},{1,0},{2,3},{3,2},{4,5},{5,4},{6,7},{7,6},{8,9},{9,8},{10,11... | collective-permute-start | bytes 1572872 | tf_op jit(solution)/shard_map/ppermute | solution.py:264
  92.8 56.5 %collective-permute-start.13 = (f32[256,2048]{1,0:T(8,128)}, f32[256,2048]{1,0:T(8,128)S(1)}, u32[]{:S(2)}, u32[]{:S(2)}) collective-permute-start(f32[256,2048]{1,0:T(8,128)} %broadcast_select_fusion), channel_id=1, source_target_pairs={{0,8},{1,9},{2,10},{3,11},{4,12},{5,13},{6,14},{7,15},{8,0},{9,1},... | collective-permute-start | bytes 6291464 | tf_op jit(solution)/shard_map/ppermute | solution.py:264
  106.6 17.9 %collective-permute-start.18 = (f32[512,256]{1,0:T(8,128)S(1)}, f32[512,256]{1,0:T(8,128)S(1)}, u32[]{:S(2)}, u32[]{:S(2)}) collective-permute-start(f32[512,256]{1,0:T(8,128)S(1)} %slice_select_fusion.1.refs_3_.refs_1_), channel_id=1, source_target_pairs={{0,2},{1,3},{2,4},{3,5},{4,6},{5,7},{8,10},{9,11},{10,12},{11,13},... | collective-permute-start | bytes 1572872 | tf_op jit(solution)/shard_map/ppermute | solution.py:264
  108.1 39.1 %collective-permute-start.21 = (f32[512,256]{1,0:T(8,128)S(1)}, f32[512,256]{1,0:T(8,128)S(1)}, u32[]{:S(2)}, u32[]{:S(2)}) collective-permute-start(f32[512,256]{1,0:T(8,128)S(1)} %slice_select_fusion.1.refs_3_.refs_1_), channel_id=1, source_target_pairs={{0,1},{1,0},{2,3},{3,2},{4,5},{5,4},{6,7},{7,6},{8,9},{9,8},{10,11... | collective-permute-start | bytes 1572872 | tf_op jit(solution)/shard_map/ppermute | solution.py:264
  125.7 20.4 %collective-permute-start.20 = (f32[512,256]{1,0:T(8,128)S(1)}, f32[512,256]{1,0:T(8,128)S(1)}, u32[]{:S(2)}, u32[]{:S(2)}) collective-permute-start(f32[512,256]{1,0:T(8,128)S(1)} %slice_select_fusion.2.refs_4_.refs_2_.refs_0_), channel_id=1, source_target_pairs={{0,2},{1,3},{2,4},{3,5},{4,6},{5,7},{8,10},{9,11},{10,12},{11,13},... | collective-permute-start | bytes 1572872 | tf_op jit(solution)/shard_map/ppermute | solution.py:264
  127.0 39.8 %collective-permute-start.23 = (f32[512,256]{1,0:T(8,128)S(1)}, f32[512,256]{1,0:T(8,128)S(1)}, u32[]{:S(2)}, u32[]{:S(2)}) collective-permute-start(f32[512,256]{1,0:T(8,128)S(1)} %slice_select_fusion.2.refs_4_.refs_2_.refs_0_), channel_id=1, source_target_pairs={{0,1},{1,0},{2,3},{3,2},{4,5},{5,4},{6,7},{7,6},{8,9},{9,8},{10,11... | collective-permute-start | bytes 1572872 | tf_op jit(solution)/shard_map/ppermute | solution.py:264
  147.2 19.6 %collective-permute-start.22 = (f32[512,256]{1,0:T(8,128)S(1)}, f32[512,256]{1,0:T(8,128)S(1)}, u32[]{:S(2)}, u32[]{:S(2)}) collective-permute-start(f32[512,256]{1,0:T(8,128)S(1)} %slice_select_fusion.3.refs_3_.refs_1_.refs_0_), channel_id=1, source_target_pairs={{0,2},{1,3},{2,4},{3,5},{4,6},{5,7},{8,10},{9,11},{10,12},{11,13},... | collective-permute-start | bytes 1572872 | tf_op jit(solution)/shard_map/ppermute | solution.py:264
  148.7 37.7 %collective-permute-start.25 = (f32[512,256]{1,0:T(8,128)S(1)}, f32[512,256]{1,0:T(8,128)S(1)}, u32[]{:S(2)}, u32[]{:S(2)}) collective-permute-start(f32[512,256]{1,0:T(8,128)S(1)} %slice_select_fusion.3.refs_3_.refs_1_.refs_0_), channel_id=1, source_target_pairs={{0,1},{1,0},{2,3},{3,2},{4,5},{5,4},{6,7},{7,6},{8,9},{9,8},{10,11... | collective-permute-start | bytes 1572872 | tf_op jit(solution)/shard_map/ppermute | solution.py:264
  166.8 19.6 %collective-permute-start.24 = (f32[512,256]{1,0:T(8,128)S(1)}, f32[512,256]{1,0:T(8,128)S(1)}, u32[]{:S(2)}, u32[]{:S(2)}) collective-permute-start(f32[512,256]{1,0:T(8,128)S(1)} %collective-permute-done.22.refs_4_.refs_2_.refs_1_), channel_id=1, source_target_pairs={{2,4},{3,5},{4,6},{5,7},{10,12},{11,13},{12,14},{13,15},{18,20},{1... | collective-permute-start | bytes 1572872 | tf_op jit(solution)/shard_map/ppermute | solution.py:264
  168.1 36.9 %collective-permute-start.27 = (f32[512,256]{1,0:T(8,128)S(1)}, f32[512,256]{1,0:T(8,128)S(1)}, u32[]{:S(2)}, u32[]{:S(2)}) collective-permute-start(f32[512,256]{1,0:T(8,128)S(1)} %collective-permute-done.22.refs_4_.refs_2_.refs_1_), channel_id=1, source_target_pairs={{2,3},{3,2},{4,5},{5,4},{6,7},{7,6},{10,11},{11,10},{12,13},{13,12... | collective-permute-start | bytes 1572872 | tf_op jit(solution)/shard_map/ppermute | solution.py:264
  186.4 18.5 %collective-permute-start.26 = (f32[512,256]{1,0:T(8,128)S(1)}, f32[512,256]{1,0:T(8,128)S(1)}, u32[]{:S(2)}, u32[]{:S(2)}) collective-permute-start(f32[512,256]{1,0:T(8,128)S(1)} %collective-permute-done.24.refs_3_.refs_2_), channel_id=1, source_target_pairs={{4,6},{5,7},{12,14},{13,15},{20,22},{21,23},{28,30},{29,31}} | collective-permute-start | bytes 1572872 | tf_op jit(solution)/shard_map/ppermute | solution.py:264
  187.7 35.7 %collective-permute-start.28 = (f32[512,256]{1,0:T(8,128)S(1)}, f32[512,256]{1,0:T(8,128)S(1)}, u32[]{:S(2)}, u32[]{:S(2)}) collective-permute-start(f32[512,256]{1,0:T(8,128)S(1)} %collective-permute-done.24.refs_3_.refs_2_), channel_id=1, source_target_pairs={{4,5},{5,4},{6,7},{7,6},{12,13},{13,12},{14,15},{15,14},{20,21},{2... | collective-permute-start | bytes 1572872 | tf_op jit(solution)/shard_map/ppermute | solution.py:264
  205.0 30.1 %collective-permute-start.29 = (f32[512,256]{1,0:T(8,128)S(1)}, f32[512,256]{1,0:T(8,128)S(1)}, u32[]{:S(2)}, u32[]{:S(2)}) collective-permute-start(f32[512,256]{1,0:T(8,128)S(1)} %collective-permute-done.26.refs_3_), channel_id=1, source_target_pairs={{6,7},{7,6},{14,15},{15,14},{22,23},{23,22},{30,31},{31,30}} | collective-permute-start | bytes 1572872 | tf_op jit(solution)/shard_map/ppermute | solution.py:264
  (26 other events, 346.8 us)
